TPU v7x, 128 devices: a whole 4x4x4 slice. The times are simulated.
128 devices in a mesh: group: 8 (over x, core), tile: 16 (over y, z).
Axes of the slice: x: 4, y: 4, z: 4, core: 2. Of those that a mesh axis runs over, the one named last changes fastest.
Arguments:
- embeddings: bfloat16 [32768, 1024], P(('group', 'tile'))
- cluster: int32 [32768], P(('group', 'tile')), may hold values from 0 to 7, as said below
Outputs:
- max_similarity: float32 [32768], P(('group', 'tile'))
Inputs may be any that keep to these rules, and one draw needn't show every extreme that they name: Among the 256 documents of one device at most 96 belong to one cluster; on every device some cluster has exactly 96, and one cluster has exactly 96 on every device of some index along tile.
All inputs are finite; a program needn't handle non-finite values.
Results may differ from a plain program's by a relative error of at most 0.00057.
Values may be sent and summed in bfloat16 or wider, within the bound.
A program may use at most 128 MiB of HBM per device.

v0:
```python
import jax
import jax.numpy as jnp
from jax import lax
from jax.sharding import PartitionSpec as P

EPS = 1e-06


def block_max(queries, query_ids, keys, key_ids):
    sims = lax.dot_general(
        queries, keys, (((1,), (1,)), ((), ())), preferred_element_type=jnp.float32
    )
    mask = query_ids[:, None] == key_ids[None, :]
    return (jnp.where(mask, sims, jnp.float32(-1.0)), mask)


def per_device(embeddings, cluster):
    n_group = lax.axis_size("group")
    doc_rows = embeddings.shape[0]
    capacity = 3 * doc_rows // n_group
    slots = n_group * capacity
    e32 = embeddings.astype(jnp.float32)
    normed = (e32 * lax.rsqrt(jnp.sum(e32 * e32, axis=1, keepdims=True) + EPS)).astype(jnp.bfloat16)
    member = (cluster[:, None] == jnp.arange(n_group, dtype=jnp.int32)[None, :]).astype(jnp.int32)
    ranking = jnp.sum((jnp.cumsum(member, axis=0) - 1) * member, axis=1)
    slot = cluster * capacity + ranking
    placed = slot[:, None] == jnp.arange(slots, dtype=jnp.int32)[None, :]
    packed = lax.dot_general(
        placed.astype(jnp.bfloat16),
        normed,
        (((0,), (0,)), ((), ())),
        preferred_element_type=jnp.float32,
    ).astype(jnp.bfloat16)
    packed_ids = jnp.max(jnp.where(placed, cluster[:, None], -1), axis=0)
    queries, query_ids = (
        lax.all_to_all(packed, "group", split_axis=0, concat_axis=0, tiled=True),
        lax.all_to_all(packed_ids, "group", split_axis=0, concat_axis=0, tiled=True),
    )
    local_index = jnp.arange(slots, dtype=jnp.int32)
    own = lax.axis_index("tile") * slots + local_index
    initial = jnp.full((slots,), -1.0, jnp.float32)
    keys = lax.all_gather(queries, "tile", axis=0, tiled=True)
    key_ids = lax.all_gather(query_ids, "tile", axis=0, tiled=True)

    def step_block(which, acc):
        key_block = lax.dynamic_slice_in_dim(keys, which * slots, slots, 0)
        id_block = lax.dynamic_slice_in_dim(key_ids, which * slots, slots, 0)
        masked, mask = block_max(queries, query_ids, key_block, id_block)
        positions = which * slots + local_index
        masked = jnp.where(own[:, None] != positions[None, :], masked, jnp.float32(-1.0))
        return jnp.maximum(acc, jnp.max(masked, axis=1))

    best = lax.fori_loop(0, keys.shape[0] // slots, step_block, initial)
    back = lax.all_to_all(best, "group", split_axis=0, concat_axis=0, tiled=True)
    return back[slot]


def solution(mesh):
    placed = (P(("group", "tile"), None), P(("group", "tile")))
    return jax.shard_map(
        per_device, mesh=mesh, in_specs=placed, out_specs=P(("group", "tile")), check_vma=False
    )
```

profile of v0, /device:TPU:1, one launch (start us, length us, event | category | flops | bytes accessed | tf_op | source)
XLA Modules:
  0.0 270.8 jit_solution(10658390183674170502)
XLA Ops:
  6.5 0.0 all-gather.3.cloned.1.call-start
  6.5 0.7 fusion.14
  7.2 0.6 reduce-window.6
  7.8 0.2 slice_reduce_fusion
  8.0 0.8 fusion.13
  8.8 0.7 compare_select_fusion
  9.5 1.2 fusion.8
  10.7 1.8 convolution_convert_fusion
  12.5 0.0 copy-start
  12.5 26.5 %all_to_all.36 = bf16[8,96,1024]{2,1,0:T(8,128)(2,1)} all-to-all(bf16[8,96,1024]{2,1,0:T(8,128)(2,1)S(1)} %bitcast.28), channel_id=1, replica_groups=mesh['group'=8,'tile'=16] {'group'}, dimensions={0} | all-to-all | bytes 3145728 | tf_op jit(solution)/shard_map/all_to_all | solution.py:36
  39.0 0.0 all-gather.3.cloned.1.call-update
  39.0 0.0 copy-done
  39.0 0.2 select_reduce_fusion
  39.2 0.7 all_to_all.24
  39.9 4.2 %all-to-all-start = ((s32[8,96,1]{1,2,0:T(1,128)}), s32[8,96,1]{1,2,0:T(1,128)S(1)}, u32[]{:S(2)}, u32[]{:S(2)}) async-start(s32[8,96,1]{1,2,0:T(1,128)} %bitcast.3), calls=%async_computation | async-start | bytes 8192 | tf_op jit(solution)/shard_map/all_to_all | solution.py:37
  44.1 4.6 %all-to-all-done = s32[8,96,1]{1,2,0:T(1,128)S(1)} async-done(((s32[8,96,1]{1,2,0:T(1,128)}), s32[8,96,1]{1,2,0:T(1,128)S(1)}, u32[]{:S(2)}, u32[]{:S(2)}) %all-to-all-start) | async-done | bytes 3104 | tf_op jit(solution)/shard_map/all_to_all | solution.py:37
  48.7 0.1 reshape.49
  48.8 0.5 broadcast.62
  49.3 0.6 reduce.10
  49.9 0.1 all_to_all.26
  49.9 21.9 %all-gather = s32[16,1,768]{2,1,0:T(1,128)S(1)} all-gather(s32[1,1,768]{2,1,0:T(1,128)S(1)} %reshape.49), channel_id=1, replica_groups=mesh['group'=8,'tile'=16] {'tile'}, dimensions={0}, use_global_device_ids=true | all-gather | bytes 52224 | tf_op jit(solution)/shard_map/all_gather | solution.py:43
  71.9 122.7 %all-gather.3.cloned.1.call-done = bf16[12288,1024]{1,0:T(8,128)(2,1)} async-done(((bf16[768,1024]{1,0:T(8,128)(2,1)}), bf16[12288,1024]{1,0:T(8,128)(2,1)}) %all-gather.3.cloned.1.call-update) | async-done | bytes 25165840 | tf_op jit(solution)/shard_map/all_gather | solution.py:42
  194.6 55.9 %while.14 = (s32[]{:T(128)}, f32[768]{0:T(1024)S(1)}, s32[768]{0:T(1024)S(1)}, s32[12288]{0:T(1024)S(1)}, bf16[12288,1024]{1,0:T(8,128)(2,1)}, /*index=5*/bf16[7...) while((s32[]{:T(128)}, f32[768]{0:T(1024)S(1)}, ...), condition=%wide.region_7.8_spmd.clone, body=%wide.region_5.7_spmd.clone.sunk | while | flops 1210910976 | bytes 3182773 | solution.py:53
  194.6 0.1 dynamic_slice.21
  194.7 3.4 %fusion.21 = f32[768]{0:T(1024)S(1)} fusion(bf16[768,1024]{1,0:T(8,128)(2,1)} %get-tuple-element.266, bf16[12288,1024]{1,0:T(8,128)(2,1)} %get-tuple-element.265, s32[]{:T(128)S(6)} %select_n.50, s32[768]{0:T(1024)S(1)} %get-tuple-element.263, s32[768]{0:T(1024)S(1)} %get-tuple-element.237, s32[768]{0:T(1024)S(1)} %dynamic_slice.21, ...), kind=kOutput, calls=%fused_computation.5.clone.1 | convolution fusion | flops 1210907904 | bytes 3161092 | tf_op jit(solution)/shard_map/while/body/eval_jaxpr/dot_general | solution.py:10
  198.1 0.1 dynamic_slice.21
  198.2 3.4 %fusion.21 = f32[768]{0:T(1024)S(1)} fusion(bf16[768,1024]{1,0:T(8,128)(2,1)} %get-tuple-element.266, bf16[12288,1024]{1,0:T(8,128)(2,1)} %get-tuple-element.265, s32[]{:T(128)S(6)} %select_n.50, s32[768]{0:T(1024)S(1)} %get-tuple-element.263, s32[768]{0:T(1024)S(1)} %get-tuple-element.237, s32[768]{0:T(1024)S(1)} %dynamic_slice.21, ...), kind=kOutput, calls=%fused_computation.5.clone.1 | convolution fusion | flops 1210907904 | bytes 3161092 | tf_op jit(solution)/shard_map/while/body/eval_jaxpr/dot_general | solution.py:10
  201.6 0.1 dynamic_slice.21
  201.7 3.4 %fusion.21 = f32[768]{0:T(1024)S(1)} fusion(bf16[768,1024]{1,0:T(8,128)(2,1)} %get-tuple-element.266, bf16[12288,1024]{1,0:T(8,128)(2,1)} %get-tuple-element.265, s32[]{:T(128)S(6)} %select_n.50, s32[768]{0:T(1024)S(1)} %get-tuple-element.263, s32[768]{0:T(1024)S(1)} %get-tuple-element.237, s32[768]{0:T(1024)S(1)} %dynamic_slice.21, ...), kind=kOutput, calls=%fused_computation.5.clone.1 | convolution fusion | flops 1210907904 | bytes 3161092 | tf_op jit(solution)/shard_map/while/body/eval_jaxpr/dot_general | solution.py:10
  205.1 0.1 dynamic_slice.21
  205.2 3.4 %fusion.21 = f32[768]{0:T(1024)S(1)} fusion(bf16[768,1024]{1,0:T(8,128)(2,1)} %get-tuple-element.266, bf16[12288,1024]{1,0:T(8,128)(2,1)} %get-tuple-element.265, s32[]{:T(128)S(6)} %select_n.50, s32[768]{0:T(1024)S(1)} %get-tuple-element.263, s32[768]{0:T(1024)S(1)} %get-tuple-element.237, s32[768]{0:T(1024)S(1)} %dynamic_slice.21, ...), kind=kOutput, calls=%fused_computation.5.clone.1 | convolution fusion | flops 1210907904 | bytes 3161092 | tf_op jit(solution)/shard_map/while/body/eval_jaxpr/dot_general | solution.py:10
  208.6 0.1 dynamic_slice.21
  208.7 3.4 %fusion.21 = f32[768]{0:T(1024)S(1)} fusion(bf16[768,1024]{1,0:T(8,128)(2,1)} %get-tuple-element.266, bf16[12288,1024]{1,0:T(8,128)(2,1)} %get-tuple-element.265, s32[]{:T(128)S(6)} %select_n.50, s32[768]{0:T(1024)S(1)} %get-tuple-element.263, s32[768]{0:T(1024)S(1)} %get-tuple-element.237, s32[768]{0:T(1024)S(1)} %dynamic_slice.21, ...), kind=kOutput, calls=%fused_computation.5.clone.1 | convolution fusion | flops 1210907904 | bytes 3161092 | tf_op jit(solution)/shard_map/while/body/eval_jaxpr/dot_general | solution.py:10
  212.1 0.1 dynamic_slice.21
  212.2 3.4 %fusion.21 = f32[768]{0:T(1024)S(1)} fusion(bf16[768,1024]{1,0:T(8,128)(2,1)} %get-tuple-element.266, bf16[12288,1024]{1,0:T(8,128)(2,1)} %get-tuple-element.265, s32[]{:T(128)S(6)} %select_n.50, s32[768]{0:T(1024)S(1)} %get-tuple-element.263, s32[768]{0:T(1024)S(1)} %get-tuple-element.237, s32[768]{0:T(1024)S(1)} %dynamic_slice.21, ...), kind=kOutput, calls=%fused_computation.5.clone.1 | convolution fusion | flops 1210907904 | bytes 3161092 | tf_op jit(solution)/shard_map/while/body/eval_jaxpr/dot_general | solution.py:10
  215.6 0.1 dynamic_slice.21
  215.7 3.4 %fusion.21 = f32[768]{0:T(1024)S(1)} fusion(bf16[768,1024]{1,0:T(8,128)(2,1)} %get-tuple-element.266, bf16[12288,1024]{1,0:T(8,128)(2,1)} %get-tuple-element.265, s32[]{:T(128)S(6)} %select_n.50, s32[768]{0:T(1024)S(1)} %get-tuple-element.263, s32[768]{0:T(1024)S(1)} %get-tuple-element.237, s32[768]{0:T(1024)S(1)} %dynamic_slice.21, ...), kind=kOutput, calls=%fused_computation.5.clone.1 | convolution fusion | flops 1210907904 | bytes 3161092 | tf_op jit(solution)/shard_map/while/body/eval_jaxpr/dot_general | solution.py:10
  219.1 0.1 dynamic_slice.21
  219.2 3.4 %fusion.21 = f32[768]{0:T(1024)S(1)} fusion(bf16[768,1024]{1,0:T(8,128)(2,1)} %get-tuple-element.266, bf16[12288,1024]{1,0:T(8,128)(2,1)} %get-tuple-element.265, s32[]{:T(128)S(6)} %select_n.50, s32[768]{0:T(1024)S(1)} %get-tuple-element.263, s32[768]{0:T(1024)S(1)} %get-tuple-element.237, s32[768]{0:T(1024)S(1)} %dynamic_slice.21, ...), kind=kOutput, calls=%fused_computation.5.clone.1 | convolution fusion | flops 1210907904 | bytes 3161092 | tf_op jit(solution)/shard_map/while/body/eval_jaxpr/dot_general | solution.py:10
  222.6 0.1 dynamic_slice.21
  222.7 3.4 %fusion.21 = f32[768]{0:T(1024)S(1)} fusion(bf16[768,1024]{1,0:T(8,128)(2,1)} %get-tuple-element.266, bf16[12288,1024]{1,0:T(8,128)(2,1)} %get-tuple-element.265, s32[]{:T(128)S(6)} %select_n.50, s32[768]{0:T(1024)S(1)} %get-tuple-element.263, s32[768]{0:T(1024)S(1)} %get-tuple-element.237, s32[768]{0:T(1024)S(1)} %dynamic_slice.21, ...), kind=kOutput, calls=%fused_computation.5.clone.1 | convolution fusion | flops 1210907904 | bytes 3161092 | tf_op jit(solution)/shard_map/while/body/eval_jaxpr/dot_general | solution.py:10
  226.1 0.1 dynamic_slice.21
  226.2 3.4 %fusion.21 = f32[768]{0:T(1024)S(1)} fusion(bf16[768,1024]{1,0:T(8,128)(2,1)} %get-tuple-element.266, bf16[12288,1024]{1,0:T(8,128)(2,1)} %get-tuple-element.265, s32[]{:T(128)S(6)} %select_n.50, s32[768]{0:T(1024)S(1)} %get-tuple-element.263, s32[768]{0:T(1024)S(1)} %get-tuple-element.237, s32[768]{0:T(1024)S(1)} %dynamic_slice.21, ...), kind=kOutput, calls=%fused_computation.5.clone.1 | convolution fusion | flops 1210907904 | bytes 3161092 | tf_op jit(solution)/shard_map/while/body/eval_jaxpr/dot_general | solution.py:10
  229.6 0.1 dynamic_slice.21
  229.7 3.4 %fusion.21 = f32[768]{0:T(1024)S(1)} fusion(bf16[768,1024]{1,0:T(8,128)(2,1)} %get-tuple-element.266, bf16[12288,1024]{1,0:T(8,128)(2,1)} %get-tuple-element.265, s32[]{:T(128)S(6)} %select_n.50, s32[768]{0:T(1024)S(1)} %get-tuple-element.263, s32[768]{0:T(1024)S(1)} %get-tuple-element.237, s32[768]{0:T(1024)S(1)} %dynamic_slice.21, ...), kind=kOutput, calls=%fused_computation.5.clone.1 | convolution fusion | flops 1210907904 | bytes 3161092 | tf_op jit(solution)/shard_map/while/body/eval_jaxpr/dot_general | solution.py:10
  233.1 0.1 dynamic_slice.21
  233.2 3.4 %fusion.21 = f32[768]{0:T(1024)S(1)} fusion(bf16[768,1024]{1,0:T(8,128)(2,1)} %get-tuple-element.266, bf16[12288,1024]{1,0:T(8,128)(2,1)} %get-tuple-element.265, s32[]{:T(128)S(6)} %select_n.50, s32[768]{0:T(1024)S(1)} %get-tuple-element.263, s32[768]{0:T(1024)S(1)} %get-tuple-element.237, s32[768]{0:T(1024)S(1)} %dynamic_slice.21, ...), kind=kOutput, calls=%fused_computation.5.clone.1 | convolution fusion | flops 1210907904 | bytes 3161092 | tf_op jit(solution)/shard_map/while/body/eval_jaxpr/dot_general | solution.py:10
  236.6 0.1 dynamic_slice.21
  236.7 3.4 %fusion.21 = f32[768]{0:T(1024)S(1)} fusion(bf16[768,1024]{1,0:T(8,128)(2,1)} %get-tuple-element.266, bf16[12288,1024]{1,0:T(8,128)(2,1)} %get-tuple-element.265, s32[]{:T(128)S(6)} %select_n.50, s32[768]{0:T(1024)S(1)} %get-tuple-element.263, s32[768]{0:T(1024)S(1)} %get-tuple-element.237, s32[768]{0:T(1024)S(1)} %dynamic_slice.21, ...), kind=kOutput, calls=%fused_computation.5.clone.1 | convolution fusion | flops 1210907904 | bytes 3161092 | tf_op jit(solution)/shard_map/while/body/eval_jaxpr/dot_general | solution.py:10
  240.1 0.1 dynamic_slice.21
  240.2 3.4 %fusion.21 = f32[768]{0:T(1024)S(1)} fusion(bf16[768,1024]{1,0:T(8,128)(2,1)} %get-tuple-element.266, bf16[12288,1024]{1,0:T(8,128)(2,1)} %get-tuple-element.265, s32[]{:T(128)S(6)} %select_n.50, s32[768]{0:T(1024)S(1)} %get-tuple-element.263, s32[768]{0:T(1024)S(1)} %get-tuple-element.237, s32[768]{0:T(1024)S(1)} %dynamic_slice.21, ...), kind=kOutput, calls=%fused_computation.5.clone.1 | convolution fusion | flops 1210907904 | bytes 3161092 | tf_op jit(solution)/shard_map/while/body/eval_jaxpr/dot_general | solution.py:10
  243.6 0.1 dynamic_slice.21
  243.7 3.4 %fusion.21 = f32[768]{0:T(1024)S(1)} fusion(bf16[768,1024]{1,0:T(8,128)(2,1)} %get-tuple-element.266, bf16[12288,1024]{1,0:T(8,128)(2,1)} %get-tuple-element.265, s32[]{:T(128)S(6)} %select_n.50, s32[768]{0:T(1024)S(1)} %get-tuple-element.263, s32[768]{0:T(1024)S(1)} %get-tuple-element.237, s32[768]{0:T(1024)S(1)} %dynamic_slice.21, ...), kind=kOutput, calls=%fused_computation.5.clone.1 | convolution fusion | flops 1210907904 | bytes 3161092 | tf_op jit(solution)/shard_map/while/body/eval_jaxpr/dot_general | solution.py:10
  247.1 0.1 dynamic_slice.21
  247.2 3.4 %fusion.21 = f32[768]{0:T(1024)S(1)} fusion(bf16[768,1024]{1,0:T(8,128)(2,1)} %get-tuple-element.266, bf16[12288,1024]{1,0:T(8,128)(2,1)} %get-tuple-element.265, s32[]{:T(128)S(6)} %select_n.50, s32[768]{0:T(1024)S(1)} %get-tuple-element.263, s32[768]{0:T(1024)S(1)} %get-tuple-element.237, s32[768]{0:T(1024)S(1)} %dynamic_slice.21, ...), kind=kOutput, calls=%fused_computation.5.clone.1 | convolution fusion | flops 1210907904 | bytes 3161092 | tf_op jit(solution)/shard_map/while/body/eval_jaxpr/dot_general | solution.py:10
  250.6 0.7 all_to_all.30
  251.3 4.9 %all-to-all-start.2 = ((f32[8,96,1]{1,2,0:T(1,128)}), f32[8,96,1]{1,2,0:T(1,128)S(1)}, u32[]{:S(2)}, u32[]{:S(2)}) async-start(f32[8,96,1]{1,2,0:T(1,128)} %bitcast.7), calls=%async_computation.2 | async-start | bytes 8192 | tf_op jit(solution)/shard_map/all_to_all | solution.py:54
  256.2 4.6 %all-to-all-done.2 = f32[8,96,1]{1,2,0:T(1,128)S(1)} async-done(((f32[8,96,1]{1,2,0:T(1,128)}), f32[8,96,1]{1,2,0:T(1,128)S(1)}, u32[]{:S(2)}, u32[]{:S(2)}) %all-to-all-start.2) | async-done | bytes 3104 | tf_op jit(solution)/shard_map/all_to_all | solution.py:54
  260.7 0.5 broadcast.63
  261.3 0.7 reduce.11
  261.9 0.1 all_to_all.32
  262.0 1.9 gather_fusion
  (37 shorter events, 0.2 us)
Async XLA Ops:
  6.5 188.1 %all-gather.3.cloned.1.call-start = ((), (), s32[]{:S(2)}) async-start(), calls=%async_computation.3 | async-start | bytes 26738688 | tf_op jit(solution)/shard_map/all_gather | solution.py:42
  12.5 26.5 %copy-start = (s32[256]{0:T(256)S(1)}, s32[256]{0:T(256)}, u32[]{:S(2)}) copy-start(s32[256]{0:T(256)} %param.5) | copy-start | bytes 3076
  39.9 8.8 %all-to-all-start = ((s32[8,96,1]{1,2,0:T(1,128)}), s32[8,96,1]{1,2,0:T(1,128)S(1)}, u32[]{:S(2)}, u32[]{:S(2)}) async-start(s32[8,96,1]{1,2,0:T(1,128)} %bitcast.3), calls=%async_computation | async-start | bytes 8192 | tf_op jit(solution)/shard_map/all_to_all | solution.py:37
  251.3 9.5 %all-to-all-start.2 = ((f32[8,96,1]{1,2,0:T(1,128)}), f32[8,96,1]{1,2,0:T(1,128)S(1)}, u32[]{:S(2)}, u32[]{:S(2)}) async-start(f32[8,96,1]{1,2,0:T(1,128)} %bitcast.7), calls=%async_computation.2 | async-start | bytes 8192 | tf_op jit(solution)/shard_map/all_to_all | solution.py:54
Sparse Core Ops, SparseCore 0:
  39.1 155.4 all-gather.2
where the time goes:
time: 271 us
  waiting for transfers between devices  132 us (49%)
  matrix products  55.6 us (21%)
  blocking collectives  48.4 us (18%)
  between operations  13.5 us (5%)
  starting transfers between devices  9.12 us (3%)
  local copies, waits for them, and re-layouts  5.99 us (2%)
  other arithmetic  5.56 us (2%)
    all_gather x1, waiting for transfers between devices, per_device(): keys = lax.all_gather(queries, 'tile', axis=0, tiled=True)  123 us
    dot_general x16, matrix products, block_max(): lax.dot_general(queries, keys, (((1,), (1,)), ((), ())), preferred_elemen...  53.9 us
    all_to_all x1, blocking collectives, per_device(): lax.all_to_all(packed, 'group', split_axis=0, concat_axis=0, tiled=True)  26.5 us
    all_gather x1, blocking collectives, per_device(): key_ids = lax.all_gather(query_ids, 'tile', axis=0, tiled=True)  21.9 us
  transfers between devices with their start and end apart: 3, of which 3 were waited for; matrix products, arithmetic and copies ran while one was open for 1% of the time, Pallas kernels for 0%

commit v1 on v0

v1 whole, which is shorter than its diff:
```python
import functools

import jax
import jax.numpy as jnp
from jax import lax
from jax.experimental import pallas as pl
from jax.experimental.pallas import tpu as pltpu
from jax.sharding import PartitionSpec as P

EPS = 1e-06
MESH = pl.DeviceIdType.MESH

TWIST = ((0, 1, 0), (0, 0, 0), (1, 0, 0))
SLOTS = (
    (0, 0, 0), (1, 0, 0), (0, 1, 0), (0, 0, 1), (3, 0, 1), (1, 3, 0), (0, 1, 3),
    (2, 0, 0), (2, 3, 0), (0, 2, 0), (0, 3, 1), (1, 0, 3), (0, 1, 2),
)
FIRST = ((0, 1, 0), (0, 2, 2), (0, 3, 4), (3, 4, 1), (1, 5, 3), (2, 6, 5))
SECOND = ((1, 7, 0), (5, 8, 1), (2, 9, 2), (3, 10, 3), (1, 11, 4), (6, 12, 5))
EARLY = ((0, (1, 2, 3, 4, 5)), (4, (1, 2, 3, 5)), (5, (1, 2, 3, 6)), (6, (1, 3, 4, 0)))
LATE = ((0, (9, 11, 7)), (2, (12, 8)), (3, (8, 9)), (4, (9, 11, 10, 12)), (5, (12, 11)), (6, (10, 8, 11)))
LAST = ((12, (7, 8)),)
SHARED = (0, 2, 3, 4, 5, 6, 12)

K = len(SLOTS)
CHUNKS = 8
AHEAD = 2


def chi(axis, parities):
    return sum(t * p for t, p in zip(TWIST[axis], parities)) % 2


def kernel(x_ref, cluster_ref, out_ref, buf, cid, rid, rowacc, colacc, outb, inb,
           arrive, shared, ids_in, ids_pair, sent, sent_pair, ids_sent, ids_pair_sent,
           res_in, res_pair_in, res_sent, res_pair_sent):
    rows = x_ref.shape[0]
    part = rows // CHUNKS
    group, tile = lax.axis_index("group"), lax.axis_index("tile")
    core = lax.rem(group, 2)
    here = (group // 2, tile // 4, lax.rem(tile, 4))
    odd = [lax.rem(h, 2) for h in here]
    sign = [1 - 2 * lax.rem(sum(t * o for t, o in zip(TWIST[a], odd)) + 0 * odd[0], 2) for a in range(3)]

    def device(chip, which):
        return (chip[0] * 2 + which, chip[1] * 4 + chip[2])

    def link(which):
        axis, step = which // 2, 1 - 2 * (which % 2)
        chip = list(here)
        chip[axis] = lax.rem(here[axis] + sign[axis] * step + 4, 4)
        return chip

    def owner(slot):
        s = SLOTS[slot]
        flip = [1 - 2 * chi(a, [v % 2 for v in s]) for a in range(3)]
        return [lax.rem(here[a] - sign[a] * (flip[a] * s[a]) + 8, 4) for a in range(3)]

    sibling = device(here, 1 - core)
    links = [device(link(w), core) for w in range(6)]

    barrier = pltpu.get_barrier_semaphore()
    partners = links + [sibling]
    for partner in partners:
        pl.semaphore_signal(barrier, inc=1, device_id=partner, device_id_type=MESH)

    e32 = x_ref[...].astype(jnp.float32)
    normed = e32 * lax.rsqrt(jnp.sum(e32 * e32, axis=1, keepdims=True) + EPS)
    buf[0, core] = normed.astype(jnp.bfloat16)
    cid[0, core] = cluster_ref[...]
    rowacc[...] = jnp.full(rowacc.shape, -1.0, jnp.float32)
    colacc[...] = jnp.full(colacc.shape, -1.0, jnp.float32)

    pl.semaphore_wait(barrier, len(partners))

    def remote(src, dst, send, recv, to):
        return pltpu.make_async_remote_copy(
            src_ref=src, dst_ref=dst, send_sem=send, recv_sem=recv, device_id=to, device_id_type=MESH
        )

    def chunk(edge, n):
        src, dst, which = edge
        piece = pl.ds(n * part, part)
        return remote(buf.at[src, core, piece], buf.at[dst, core, piece], sent.at[dst], arrive.at[dst, n], links[which])

    def across(slot, n):
        piece = pl.ds(n * part, part)
        return remote(buf.at[slot, core, piece], buf.at[slot, core, piece], sent_pair.at[slot], shared.at[slot], sibling)

    def whole(slot):
        return remote(buf.at[slot, core], buf.at[slot, core], sent_pair.at[slot], shared.at[slot], sibling)

    def ids_across():
        return remote(cid.at[0, core], cid.at[0, core], ids_pair_sent, ids_pair, sibling)

    def ids(edge):
        src, dst, which = edge
        return remote(cid.at[src], cid.at[dst], ids_sent.at[dst], ids_in.at[dst], links[which])

    first_of = {e[2]: e for e in FIRST}
    second_of = {e[2]: e for e in SECOND}
    eager = [w for w in range(6) if first_of[w][0] == 0]
    relayed = [e for e in FIRST if e[0] != 0]

    def queue(n):
        for w in eager:
            if n < CHUNKS:
                chunk(first_of[w], n).start()
            elif n < 2 * CHUNKS:
                chunk(second_of[w], n - CHUNKS).start()

    def got(slot, n):
        chunk((0, slot, 0), n).wait_recv()
        if slot in SHARED:
            across(slot, n).start()

    def row_ids(slot):
        wide = jnp.broadcast_to(cid[slot, core], (128, rows))
        rid[slot] = wide.T

    def compare(columns, which, begin, count, own=False):
        a = jnp.concatenate([buf[i, core, pl.ds(begin, count)] for i in which], axis=0)
        b = jnp.concatenate([buf[columns, 0], buf[columns, 1]], axis=0)
        s = lax.dot_general(a, b, (((1,), (1,)), ((), ())), preferred_element_type=jnp.float32)
        left = jnp.concatenate([rid[i, pl.ds(begin, count)] for i in which], axis=0)
        mask = jnp.concatenate([left] * (2 * rows // 128), axis=1) == jnp.concatenate(
            [cid[columns, 0], cid[columns, 1]], axis=1
        )
        if own:
            at = lax.broadcasted_iota(jnp.int32, s.shape, 0) + core * rows
            mask = mask & (at != lax.broadcasted_iota(jnp.int32, s.shape, 1))
        s = jnp.where(mask, s, -1.0)
        best = s[:, :128]
        for q in range(1, 2 * rows // 128):
            best = jnp.maximum(best, s[:, 128 * q : 128 * q + 128])
        for n, i in enumerate(which):
            rowacc[i, pl.ds(begin, count)] = jnp.maximum(
                rowacc[i, pl.ds(begin, count)], best[n * count : (n + 1) * count]
            )
        if not own:
            total = jnp.max(s.reshape(s.shape[0] // 8, 8, s.shape[1]), axis=0)
            colacc[columns] = jnp.maximum(colacc[columns], total)

    ids_across().start()
    for n in range(AHEAD):
        queue(n)
    for n in range(CHUNKS):
        across(0, n).start()
    ids_across().wait()
    for e in FIRST:
        if e[0] == 0:
            ids(e).start()
    for e in FIRST:
        if e[0] == 0:
            ids((0, e[1], 0)).wait_recv()
            for f in FIRST + SECOND:
                if f[0] == e[1]:
                    ids(f).start()
    row_ids(0)
    for e in FIRST:
        if e[0] == 0:
            row_ids(e[1])

    work = {}
    work[0] = [lambda: compare(0, (0,), 0, rows, own=True)]
    for t, (j, which) in enumerate(EARLY):
        work[CHUNKS + 1 + t] = [functools.partial(compare, j, which, 0, rows)]
    half = rows // 2
    for t, (j, which) in enumerate(LATE):
        work.setdefault(CHUNKS + 5 + t // 2, []).append(functools.partial(compare, j, which, 0, half))

    for step in range(2 * CHUNKS + 1):
        queue(step + AHEAD)
        if step < CHUNKS:
            for e in FIRST:
                if e[0] == 0:
                    got(e[1], step)
                    for f in relayed:
                        if f[0] == e[1]:
                            chunk(f, step).start()
        if 1 <= step <= CHUNKS:
            for f in relayed:
                got(f[1], step - 1)
        if CHUNKS <= step < 2 * CHUNKS:
            for w in range(6):
                if w not in eager:
                    chunk(second_of[w], step - CHUNKS).start()
            for w in eager:
                got(second_of[w][1], step - CHUNKS)
        if step > CHUNKS:
            for w in range(6):
                if w not in eager:
                    got(second_of[w][1], step - CHUNKS - 1)
        if step == 0:
            whole(0).wait_recv()
        if step == 1:
            for f in relayed:
                ids((0, f[1], 0)).wait_recv()
                for e in SECOND:
                    if e[0] == f[1]:
                        ids(e).start()
                row_ids(f[1])
        if step == 2:
            for e in SECOND:
                ids((0, e[1], 0)).wait_recv()
                row_ids(e[1])
        if step == CHUNKS + 1:
            for slot in SHARED[1:-1]:
                whole(slot).wait_recv()
        for job in work.get(step, ()):
            job()
    for j, which in LATE:
        compare(j, which, half, rows - half)
    whole(SHARED[-1]).wait_recv()
    for j, which in LAST:
        compare(j, which, 0, rows)

    def result(slot, which):
        return remote(outb.at[slot, which], inb.at[slot, core], res_sent, res_in, device(owner(slot), which))

    def result_pair():
        return remote(outb.at[0, 1 - core], inb.at[0, core], res_pair_sent, res_pair_in, sibling)

    for slot in range(K):
        down = jnp.max(colacc[slot], axis=0, keepdims=True)
        outb[slot, 0] = down[:, :rows]
        outb[slot, 1] = down[:, rows:]
        along = jnp.max(rowacc[slot].T, axis=0, keepdims=True)
        outb[slot, core] = jnp.maximum(outb[slot, core], along)
        if slot == 0:
            result_pair().start()
        else:
            for which in range(2):
                result(slot, which).start()
    result_pair().wait()
    everything = pltpu.make_async_remote_copy(
        src_ref=outb.at[pl.ds(1, K - 1)], dst_ref=inb.at[pl.ds(1, K - 1)], send_sem=res_sent, recv_sem=res_in,
        device_id=sibling, device_id_type=MESH,
    )
    everything.wait_recv()
    best = jnp.maximum(outb[0, core], inb[0, 1 - core])
    best = jnp.maximum(best, jnp.max(jnp.max(inb[pl.ds(1, K - 1)], axis=0), axis=0))
    out_ref[...] = jnp.maximum(best, -1.0)

    everything.wait_send()
    for src, dst, which in FIRST + SECOND:
        ids((src, dst, which)).wait_send()
        remote(buf.at[src, core], buf.at[dst, core], sent.at[dst], arrive.at[dst, 0], links[which]).wait_send()
    for slot in SHARED:
        whole(slot).wait_send()


def per_device(embeddings, cluster):
    rows, width = embeddings.shape
    dma = pltpu.SemaphoreType.DMA
    best = pl.pallas_call(
        kernel,
        out_shape=jax.ShapeDtypeStruct((1, rows), jnp.float32),
        in_specs=[pl.BlockSpec(memory_space=pltpu.VMEM)] * 2,
        out_specs=pl.BlockSpec(memory_space=pltpu.VMEM),
        scratch_shapes=[
            pltpu.VMEM((K, 2, rows, width), jnp.bfloat16),
            pltpu.VMEM((K, 2, 1, rows), jnp.int32),
            pltpu.VMEM((K, rows, 128), jnp.int32),
            pltpu.VMEM((K, rows, 128), jnp.float32),
            pltpu.VMEM((K, 8, 2 * rows), jnp.float32),
            pltpu.VMEM((K, 2, 1, rows), jnp.float32),
            pltpu.VMEM((K, 2, 1, rows), jnp.float32),
            dma((K, CHUNKS)), dma((K,)), dma((K,)), dma, dma((K,)), dma((K,)), dma((K,)), dma,
            dma, dma, dma, dma,
        ],
        compiler_params=pltpu.CompilerParams(
            collective_id=0, has_side_effects=True, vmem_limit_bytes=56 * 2**20
        ),
    )(embeddings, cluster.reshape(1, rows))
    return best.reshape(rows)


def solution(mesh):
    placed = (P(("group", "tile"), None), P(("group", "tile")))
    return jax.shard_map(
        per_device, mesh=mesh, in_specs=placed, out_specs=P(("group", "tile")), check_vma=False
    )
```

time: 271 us -> 66.2 us (0.24)
  waiting for transfers between devices: 132 us -> 0 us
  Pallas kernels: 0 us -> 64.9 us
  matrix products: 55.6 us -> 0 us
  blocking collectives: 48.4 us -> 0 us
  between operations: 13.5 us -> 0.02 us
  starting transfers between devices: 9.12 us -> 0 us
  other arithmetic: 5.56 us -> 0 us
  local copies, waits for them, and re-layouts: 5.99 us -> 1.22 us
    all_gather x1 -> x0, waiting for transfers between devices: 123 us -> none  [per_device(): keys = lax.all_gather(queries, 'tile', axis=0, tiled=True)]
    pallas_call x0 -> x1, Pallas kernels: none -> 64.9 us  [per_device(): pl.pallas_call(kernel, out_shape=jax.ShapeDtypeStruct((1, rows), jnp.floa...]
    dot_general x17 -> x0, matrix products: 55.6 us -> none  [the longest x16 53.9 us: block_max(): lax.dot_general(queries, keys, (((1,), (1,)), ((), ())), preferred_elemen...]
    all_to_all x1 -> x0, blocking collectives: 26.5 us -> none  [per_device(): lax.all_to_all(packed, 'group', split_axis=0, concat_axis=0, tiled=True)]
    all_gather x1 -> x0, blocking collectives: 21.9 us -> none  [per_device(): key_ids = lax.all_gather(query_ids, 'tile', axis=0, tiled=True)]
    all_to_all x2 -> x0, waiting for transfers between devices: 9.16 us -> none  [the longest x1 4.59 us: per_device(): lax.all_to_all(packed_ids, 'group', split_axis=0, concat_axis=0, tiled=True)]
    all_to_all x2 -> x0, starting transfers between devices: 9.12 us -> none  [the longest x1 4.91 us: per_device(): lax.all_to_all(best, 'group', split_axis=0, concat_axis=0, tiled=True)]
  transfers between devices with their start and end apart: 3 -> 0, of which waited for: 3 -> 0; matrix products, arithmetic and copies ran while one was open for 1% -> 0% of each run, Pallas kernels for 0% -> 0%
where the time goes in v1:
time: 66.2 us; the launch traced here: 66.1 us
  Pallas kernels  64.9 us (98%)
  local copies, waits for them, and re-layouts  1.22 us (2%)
    pallas_call x1, Pallas kernels, per_device(): pl.pallas_call(kernel, out_shape=jax.ShapeDtypeStruct((1, rows), jnp.floa...  64.9 us

profile of v1, /device:TPU:1, one launch (start us, length us, event | category | flops | bytes accessed | tf_op | source)
XLA Modules:
  0.0 66.1 jit_solution(7795132163680064305)
XLA Ops:
  0.0 64.9 %shard_map.28 = f32[1,256]{1,0:T(1,128)} custom-call(bf16[256,1024]{1,0:T(8,128)(2,1)} %x_ref.1, s32[1,256]{1,0:T(1,128)} %bitcast.3), custom_call_target="tpu_custom_call" | custom-call | tf_op jit(solution)/shard_map/pallas_call | solution.py:256
  64.9 0.0 copy-start
  64.9 0.7 copy-done
  65.5 0.6 copy.4
Async XLA Ops:
  64.9 0.7 %copy-start = (f32[1,256]{1,0:T(1,128)S(1)}, f32[1,256]{1,0:T(1,128)}, u32[]{:S(2)}) copy-start(f32[1,256]{1,0:T(1,128)} %shard_map.28) | copy-start | bytes 3076

commit v2 on v1

--- a/solution.py
+++ b/solution.py
@@ -24,7 +24,8 @@
 
 K = len(SLOTS)
 CHUNKS = 8
-AHEAD = 2
+AHEAD = 4
+LAG = 3
 
 
 def chi(axis, parities):
@@ -90,12 +91,21 @@
     def whole(slot):
         return remote(buf.at[slot, core], buf.at[slot, core], sent_pair.at[slot], shared.at[slot], sibling)
 
-    def ids_across():
-        return remote(cid.at[0, core], cid.at[0, core], ids_pair_sent, ids_pair, sibling)
+    def ids_across(slot):
+        return remote(cid.at[slot, core], cid.at[slot, core], ids_pair_sent.at[slot], ids_pair.at[slot], sibling)
 
     def ids(edge):
         src, dst, which = edge
-        return remote(cid.at[src], cid.at[dst], ids_sent.at[dst], ids_in.at[dst], links[which])
+        return remote(cid.at[src, core], cid.at[dst, core], ids_sent.at[dst], ids_in.at[dst], links[which])
+
+    def got_ids(slot):
+        ids((0, slot, 0)).wait_recv()
+        for e in FIRST + SECOND:
+            if e[0] == slot:
+                ids(e).start()
+        if slot in SHARED:
+            ids_across(slot).start()
+        row_ids(slot)
 
     first_of = {e[2]: e for e in FIRST}
     second_of = {e[2]: e for e in SECOND}
@@ -141,35 +151,25 @@
             total = jnp.max(s.reshape(s.shape[0] // 8, 8, s.shape[1]), axis=0)
             colacc[columns] = jnp.maximum(colacc[columns], total)
 
-    ids_across().start()
+    for e in FIRST + SECOND:
+        if e[0] == 0:
+            ids(e).start()
     for n in range(AHEAD):
         queue(n)
+    ids_across(0).start()
     for n in range(CHUNKS):
         across(0, n).start()
-    ids_across().wait()
-    for e in FIRST:
-        if e[0] == 0:
-            ids(e).start()
-    for e in FIRST:
-        if e[0] == 0:
-            ids((0, e[1], 0)).wait_recv()
-            for f in FIRST + SECOND:
-                if f[0] == e[1]:
-                    ids(f).start()
     row_ids(0)
-    for e in FIRST:
-        if e[0] == 0:
-            row_ids(e[1])
 
     work = {}
-    work[0] = [lambda: compare(0, (0,), 0, rows, own=True)]
+    work[1] = [lambda: compare(0, (0,), 0, rows, own=True)]
     for t, (j, which) in enumerate(EARLY):
-        work[CHUNKS + 1 + t] = [functools.partial(compare, j, which, 0, rows)]
+        work[CHUNKS + LAG + t] = [functools.partial(compare, j, which, 0, rows)]
     half = rows // 2
     for t, (j, which) in enumerate(LATE):
-        work.setdefault(CHUNKS + 5 + t // 2, []).append(functools.partial(compare, j, which, 0, half))
-
-    for step in range(2 * CHUNKS + 1):
+        work.setdefault(CHUNKS + LAG + 4 + t // 2, []).append(functools.partial(compare, j, which, 0, half))
+
+    for step in range(2 * CHUNKS + LAG):
         queue(step + AHEAD)
         if step < CHUNKS:
             for e in FIRST:
@@ -178,39 +178,41 @@
                     for f in relayed:
                         if f[0] == e[1]:
                             chunk(f, step).start()
-        if 1 <= step <= CHUNKS:
+        if LAG <= step < CHUNKS + LAG:
             for f in relayed:
-                got(f[1], step - 1)
+                got(f[1], step - LAG)
         if CHUNKS <= step < 2 * CHUNKS:
             for w in range(6):
                 if w not in eager:
                     chunk(second_of[w], step - CHUNKS).start()
             for w in eager:
                 got(second_of[w][1], step - CHUNKS)
-        if step > CHUNKS:
+        if step >= CHUNKS + LAG:
             for w in range(6):
                 if w not in eager:
-                    got(second_of[w][1], step - CHUNKS - 1)
+                    got(second_of[w][1], step - CHUNKS - LAG)
         if step == 0:
+            for e in FIRST:
+                if e[0] == 0:
+                    got_ids(e[1])
+        if step == 1:
+            ids_across(0).wait_recv()
             whole(0).wait_recv()
-        if step == 1:
+        if step == LAG:
             for f in relayed:
-                ids((0, f[1], 0)).wait_recv()
-                for e in SECOND:
-                    if e[0] == f[1]:
-                        ids(e).start()
-                row_ids(f[1])
-        if step == 2:
+                got_ids(f[1])
+        if step == CHUNKS:
             for e in SECOND:
-                ids((0, e[1], 0)).wait_recv()
-                row_ids(e[1])
-        if step == CHUNKS + 1:
+                got_ids(e[1])
+        if step == CHUNKS + LAG:
             for slot in SHARED[1:-1]:
+                ids_across(slot).wait_recv()
                 whole(slot).wait_recv()
         for job in work.get(step, ()):
             job()
     for j, which in LATE:
         compare(j, which, half, rows - half)
+    ids_across(SHARED[-1]).wait_recv()
     whole(SHARED[-1]).wait_recv()
     for j, which in LAST:
         compare(j, which, 0, rows)
@@ -240,22 +242,23 @@
     everything.wait_recv()
     best = jnp.maximum(outb[0, core], inb[0, 1 - core])
     best = jnp.maximum(best, jnp.max(jnp.max(inb[pl.ds(1, K - 1)], axis=0), axis=0))
-    out_ref[...] = jnp.maximum(best, -1.0)
+    out_ref[...] = jnp.maximum(best, -1.0)[0]
 
     everything.wait_send()
     for src, dst, which in FIRST + SECOND:
         ids((src, dst, which)).wait_send()
         remote(buf.at[src, core], buf.at[dst, core], sent.at[dst], arrive.at[dst, 0], links[which]).wait_send()
     for slot in SHARED:
+        ids_across(slot).wait_send()
         whole(slot).wait_send()
 
 
 def per_device(embeddings, cluster):
     rows, width = embeddings.shape
     dma = pltpu.SemaphoreType.DMA
-    best = pl.pallas_call(
+    return pl.pallas_call(
         kernel,
-        out_shape=jax.ShapeDtypeStruct((1, rows), jnp.float32),
+        out_shape=jax.ShapeDtypeStruct((rows,), jnp.float32),
         in_specs=[pl.BlockSpec(memory_space=pltpu.VMEM)] * 2,
         out_specs=pl.BlockSpec(memory_space=pltpu.VMEM),
         scratch_shapes=[
@@ -266,14 +269,13 @@
             pltpu.VMEM((K, 8, 2 * rows), jnp.float32),
             pltpu.VMEM((K, 2, 1, rows), jnp.float32),
             pltpu.VMEM((K, 2, 1, rows), jnp.float32),
-            dma((K, CHUNKS)), dma((K,)), dma((K,)), dma, dma((K,)), dma((K,)), dma((K,)), dma,
+            dma((K, CHUNKS)), dma((K,)), dma((K,)), dma((K,)), dma((K,)), dma((K,)), dma((K,)), dma((K,)),
             dma, dma, dma, dma,
         ],
         compiler_params=pltpu.CompilerParams(
             collective_id=0, has_side_effects=True, vmem_limit_bytes=56 * 2**20
         ),
     )(embeddings, cluster.reshape(1, rows))
-    return best.reshape(rows)
 
 
 def solution(mesh):

time: 66.2 us -> 50.1 us (0.76)
  Pallas kernels: 64.9 us -> 48.7 us
    pallas_call x1, Pallas kernels: 64.9 us -> 48.7 us  [per_device(): pl.pallas_call(kernel, out_shape=jax.ShapeDtypeStruct((rows,), jnp.float3...]
where the time goes in v2:
time: 50.1 us; the launch traced here: 50 us
  Pallas kernels  48.7 us (97%)
  local copies, waits for them, and re-layouts  1.24 us (2%)
    pallas_call x1, Pallas kernels, per_device(): pl.pallas_call(kernel, out_shape=jax.ShapeDtypeStruct((rows,), jnp.float3...  48.7 us
    unnamed x1, local copies, waits for them, and re-layouts  1.24 us

profile of v2, /device:TPU:1, one launch (start us, length us, event | category | flops | bytes accessed | tf_op | source)
XLA Modules:
  0.0 50.0 jit_solution(14124663236333830626)
XLA Ops:
  0.0 48.7 %shard_map.28 = f32[256]{0:T(256)} custom-call(bf16[256,1024]{1,0:T(8,128)(2,1)} %x_ref.1, s32[1,256]{1,0:T(1,128)} %bitcast.1), custom_call_target="tpu_custom_call" | custom-call | tf_op jit(solution)/shard_map/pallas_call | solution.py:259
  48.7 1.2 %copy.4 = f32[256]{0:T(256)} copy(f32[256]{0:T(256)} %shard_map.28) | data formatting | bytes 2048

commit v3 on v2

v3 whole, which is shorter than its diff:
```python
import functools

import jax
import jax.numpy as jnp
from jax import lax
from jax.experimental import pallas as pl
from jax.experimental.pallas import tpu as pltpu
from jax.sharding import PartitionSpec as P

EPS = 1e-06
MESH = pl.DeviceIdType.MESH

SLOTS = (
    (0, 0, 0), (1, 0, 0), (3, 0, 0), (0, 1, 0), (0, 0, 1), (1, 3, 0), (3, 0, 3),
    (1, 1, 0), (3, 1, 0), (0, 2, 0), (0, 0, 2), (1, 2, 0), (3, 0, 2),
)
FIRST = ((0, 1, 0), (0, 2, 1), (0, 3, 2), (0, 4, 4), (1, 5, 3), (2, 6, 5))
SECOND = ((3, 7, 0), (3, 8, 1), (3, 9, 2), (4, 10, 4), (5, 11, 3), (6, 12, 5))
NEAR = ((4, (0, 2, 3)), (3, (0, 2, 1)), (1, (0, 2, 4)))
RELAYED = ((5, (3, 4, 2)), (6, (4, 3, 1, 5)))
FAR = ((0, (10, 9)), (4, (9, 7, 8)), (3, (10,)), (5, (10, 8)), (6, (8, 9, 7)))
LAST = ((4, (11,)), (6, (11,)))
LAST_FULL = ((10, (9, 7, 11)), (7, (12,)))
LAST_EITHER = ((1, 11), (12,))
ARRIVING = ((1, 2, 3, 4), (5, 6), (7, 8, 9, 10, 11, 12))
TOGETHER = ((0,), (1, 3, 4), (5, 6), (7, 10, 11))
SHARED = (0, 1, 3, 4, 5, 6, 7, 10, 11)

K = len(SLOTS)
BOUNDS = (0, 32, 64, 96, 128, 160, 192, 224, 256)
CHUNKS = len(BOUNDS) - 1
HALFWAY = 4
AHEAD = 3


def kernel(x_ref, cluster_ref, out_ref, buf, cid, rid, rowacc, colacc, outb, inb,
           arrive, shared, ids_in, ids_pair, sent, sent_pair, ids_sent, ids_pair_sent,
           res_in, res_pair_in, res_sent, res_pair_sent):
    rows = x_ref.shape[0]
    half = rows // 2
    group, tile = lax.axis_index("group"), lax.axis_index("tile")
    core = lax.rem(group, 2)
    here = (group // 2, tile // 4, lax.rem(tile, 4))
    def device(chip, which):
        return (chip[0] * 2 + which, chip[1] * 4 + chip[2])

    def link(which):
        axis, step = which // 2, 1 - 2 * (which % 2)
        chip = list(here)
        chip[axis] = lax.rem(here[axis] + step + 4, 4)
        return chip

    def owner(slot):
        return [lax.rem(h - s + 4, 4) for h, s in zip(here, SLOTS[slot])]

    sibling = device(here, 1 - core)
    links = [device(link(w), core) for w in range(6)]

    barrier = pltpu.get_barrier_semaphore()
    partners = links + [sibling]
    for partner in partners:
        pl.semaphore_signal(barrier, inc=1, device_id=partner, device_id_type=MESH)

    e32 = x_ref[...].astype(jnp.float32)
    normed = e32 * lax.rsqrt(jnp.sum(e32 * e32, axis=1, keepdims=True) + EPS)
    buf[0, core] = normed.astype(jnp.bfloat16)
    cid[0, core] = cluster_ref[...]
    rowacc[...] = jnp.full(rowacc.shape, -1.0, jnp.float32)
    colacc[...] = jnp.full(colacc.shape, -1.0, jnp.float32)

    pl.semaphore_wait(barrier, len(partners))

    def remote(src, dst, send, recv, to):
        return pltpu.make_async_remote_copy(
            src_ref=src, dst_ref=dst, send_sem=send, recv_sem=recv, device_id=to, device_id_type=MESH
        )

    def piece(begin, end):
        return pl.ds(begin, end - begin)

    def move(edge, rows_of, sem):
        src, dst, which = edge
        return remote(buf.at[src, core, rows_of], buf.at[dst, core, rows_of], sent, sem, links[which])

    def chunk(edge, n):
        dst = edge[1]
        sem = arrive.at[(dst - 1) * CHUNKS + n if dst in (1, 2) else 2 * CHUNKS + 2 * (dst - 3) + n // HALFWAY]
        return move(edge, piece(BOUNDS[n], BOUNDS[n + 1]), sem)

    def part(edge, h):
        return move(edge, piece(h * half, (h + 1) * half), arrive.at[2 * CHUNKS + 2 * (edge[1] - 3) + h])

    def got(slot, h):
        part((0, slot, 0), h).wait_recv()

    def across(slot, h):
        rows_of = piece(h * half, (h + 1) * half)
        return remote(buf.at[slot, core, rows_of], buf.at[slot, core, rows_of], sent_pair, shared.at[slot], sibling)

    def whole(slot):
        return remote(buf.at[slot, core], buf.at[slot, core], sent_pair, shared.at[slot], sibling)

    def whole_shared(*slots):
        some = pl.ds(0, len(slots))
        remote(cid.at[some, core], cid.at[some, core], ids_pair_sent, ids_pair.at[slots[0]], sibling).wait_recv()
        for slot in slots:
            whole(slot).wait_recv()

    def ids_across(slot):
        group = next(g for g in TOGETHER if slot in g)[0]
        return remote(cid.at[slot, core], cid.at[slot, core], ids_pair_sent, ids_pair.at[group], sibling)

    def ids(edge):
        src, dst, which = edge
        group = next(g for g in ARRIVING if dst in g)[0]
        return remote(cid.at[src, core], cid.at[dst, core], ids_sent, ids_in.at[group], links[which])

    def got_ids(*slots):
        some = pl.ds(slots[0], len(slots))
        remote(cid.at[some, core], cid.at[some, core], ids_sent, ids_in.at[slots[0]], sibling).wait_recv()
        for slot in slots:
            for e in FIRST + SECOND:
                if e[0] == slot:
                    ids(e).start()
            if slot in SHARED:
                ids_across(slot).start()
        for slot in slots:
            row_ids(slot)

    edge_to = {e[1]: e for e in FIRST + SECOND}

    def row_ids(slot):
        wide = jnp.broadcast_to(cid[slot, core], (128, rows))
        rid[slot] = wide.T

    def compare(columns, pieces, own=False):
        a = jnp.concatenate([buf[i, core, pl.ds(begin, count)] for i, begin, count in pieces], axis=0)
        b = jnp.concatenate([buf[columns, 0], buf[columns, 1]], axis=0)
        s = lax.dot_general(a, b, (((1,), (1,)), ((), ())), preferred_element_type=jnp.float32)
        left = jnp.concatenate([rid[i, pl.ds(begin, count)] for i, begin, count in pieces], axis=0)
        mask = jnp.concatenate([left] * (2 * rows // 128), axis=1) == jnp.concatenate(
            [cid[columns, 0], cid[columns, 1]], axis=1
        )
        if own:
            at = lax.broadcasted_iota(jnp.int32, s.shape, 0) + core * rows
            mask = mask & (at != lax.broadcasted_iota(jnp.int32, s.shape, 1))
        s = jnp.where(mask, s, -1.0)
        best = s[:, :128]
        for q in range(1, 2 * rows // 128):
            best = jnp.maximum(best, s[:, 128 * q : 128 * q + 128])
        row = 0
        for i, begin, count in pieces:
            rowacc[i, pl.ds(begin, count)] = jnp.maximum(rowacc[i, pl.ds(begin, count)], best[row : row + count])
            row += count
        if not own:
            total = jnp.max(s.reshape(s.shape[0] // 8, 8, s.shape[1]), axis=0)
            colacc[columns] = jnp.maximum(colacc[columns], total)

    def full(which):
        return [(i, 0, rows) for i in which]

    def halves(which, h):
        return [(i, h * half, half) for i in which]

    for dst in (1, 2, 3, 4):
        ids(edge_to[dst]).start()
    for n in range(AHEAD):
        for dst in (1, 2):
            chunk(edge_to[dst], n).start()
        if n == 0:
            for dst in (3, 4):
                part(edge_to[dst], 0).start()
    ids_across(0).start()
    for h in range(2):
        across(0, h).start()
    row_ids(0)

    for n in range(CHUNKS):
        for dst in (1, 2):
            if n + AHEAD < CHUNKS:
                chunk(edge_to[dst], n + AHEAD).start()
        if n + AHEAD == CHUNKS:
            for dst in (7, 8):
                part(edge_to[dst], 0).start()
        for src, dst in ((1, 5), (2, 6)):
            chunk(edge_to[src], n).wait_recv()
            chunk(edge_to[dst], n).start()
        if n == 0:
            got_ids(1, 2, 3, 4)
        if n == 1:
            for dst in (3, 4):
                part(edge_to[dst], 1).start()
            whole_shared(0)
            compare(0, full((0,)), own=True)
        if n == HALFWAY:
            for dst in (3, 4):
                got(dst, 0)
            for dst in (9, 10):
                part(edge_to[dst], 0).start()
            for dst in (1, 3, 4):
                across(dst, 0).start()
            got_ids(5, 6)
    for dst in (5, 6):
        got(dst, 0)
    for dst in (11, 12):
        part(edge_to[dst], 0).start()
    for dst in (3, 4):
        got(dst, 1)
    for dst in (7, 8, 9, 10):
        part(edge_to[dst], 1).start()
    for dst in (1, 3, 4):
        across(dst, 1).start()
    for dst in (5, 6):
        across(dst, 0).start()
    whole_shared(1, 3, 4)
    compare(NEAR[0][0], full(NEAR[0][1]))
    for dst in (5, 6):
        got(dst, 1)
    for dst in (11, 12):
        part(edge_to[dst], 1).start()
    for dst in (5, 6):
        across(dst, 1).start()
    got_ids(7, 8, 9, 10, 11, 12)
    for j, which in NEAR[1:]:
        compare(j, full(which))
    whole_shared(5, 6)
    for j, which in RELAYED:
        compare(j, full(which))

    for h in range(2):
        for dst in (7, 8, 9, 10):
            got(dst, h)
        for dst in (7, 10):
            across(dst, h).start()
        for j, which in FAR:
            compare(j, halves(which, h))
        for dst in (11, 12):
            got(dst, h)
        across(11, h).start()
        for j, which in LAST:
            compare(j, halves(which, h))
    whole_shared(7, 10, 11)
    for j, which in LAST_FULL:
        compare(j, full(which))
    either, which = LAST_EITHER
    compare(jnp.where(here[0] // 2 == 0, *either), full(which))

    def result(slot, which):
        return remote(outb.at[slot, which], inb.at[slot, core], res_sent, res_in, device(owner(slot), which))

    def result_pair():
        return remote(outb.at[0, 1 - core], inb.at[0, core], res_pair_sent, res_pair_in, sibling)

    for slot in range(K):
        down = jnp.max(colacc[slot], axis=0, keepdims=True)
        outb[slot, 0] = down[:, :rows]
        outb[slot, 1] = down[:, rows:]
        along = jnp.max(rowacc[slot].T, axis=0, keepdims=True)
        outb[slot, core] = jnp.maximum(outb[slot, core], along)
        if slot == 0:
            result_pair().start()
        else:
            for which in range(2):
                result(slot, which).start()
    result_pair().wait()
    everything = pltpu.make_async_remote_copy(
        src_ref=outb.at[pl.ds(1, K - 1)], dst_ref=inb.at[pl.ds(1, K - 1)], send_sem=res_sent, recv_sem=res_in,
        device_id=sibling, device_id_type=MESH,
    )
    everything.wait_recv()
    best = jnp.maximum(outb[0, core], inb[0, 1 - core])
    best = jnp.maximum(best, jnp.max(jnp.max(inb[pl.ds(1, K - 1)], axis=0), axis=0))
    out_ref[...] = jnp.maximum(best, -1.0)[0]

    everything.wait_send()
    every, across_all = pl.ds(0, len(FIRST + SECOND)), pl.ds(0, len(SHARED))
    remote(cid.at[every, core], cid.at[every, core], ids_sent, ids_in.at[0], sibling).wait_send()
    remote(buf.at[every, core], buf.at[every, core], sent, arrive.at[0], sibling).wait_send()
    remote(cid.at[across_all, core], cid.at[across_all, core], ids_pair_sent, ids_pair.at[0], sibling).wait_send()
    remote(buf.at[across_all, core], buf.at[across_all, core], sent_pair, shared.at[0], sibling).wait_send()


def per_device(embeddings, cluster):
    rows, width = embeddings.shape
    dma = pltpu.SemaphoreType.DMA
    return pl.pallas_call(
        kernel,
        out_shape=jax.ShapeDtypeStruct((rows,), jnp.float32),
        in_specs=[pl.BlockSpec(memory_space=pltpu.VMEM)] * 2,
        out_specs=pl.BlockSpec(memory_space=pltpu.VMEM),
        scratch_shapes=[
            pltpu.VMEM((K, 2, rows, width), jnp.bfloat16),
            pltpu.VMEM((K, 2, 1, rows), jnp.int32),
            pltpu.VMEM((K, rows, 128), jnp.int32),
            pltpu.VMEM((K, rows, 128), jnp.float32),
            pltpu.VMEM((K, 8, 2 * rows), jnp.float32),
            pltpu.VMEM((K, 2, 1, rows), jnp.float32),
            pltpu.VMEM((K, 2, 1, rows), jnp.float32),
            dma((2 * CHUNKS + 2 * (K - 3),)), dma((K,)), dma((K,)), dma((K,)), dma, dma, dma, dma,
            dma, dma, dma, dma,
        ],
        compiler_params=pltpu.CompilerParams(
            collective_id=0, has_side_effects=True, vmem_limit_bytes=56 * 2**20
        ),
    )(embeddings, cluster.reshape(1, rows))


def solution(mesh):
    placed = (P(("group", "tile"), None), P(("group", "tile")))
    return jax.shard_map(
        per_device, mesh=mesh, in_specs=placed, out_specs=P(("group", "tile")), check_vma=False
    )
```

time: 50.1 us -> 46.3 us (0.924)
  Pallas kernels: 48.7 us -> 44.9 us
    pallas_call x1, Pallas kernels: 48.7 us -> 44.9 us  [per_device(): pl.pallas_call(kernel, out_shape=jax.ShapeDtypeStruct((rows,), jnp.float3...]
where the time goes in v3:
time: 46.3 us; the launch traced here: 46.2 us
  Pallas kernels  44.9 us (97%)
  local copies, waits for them, and re-layouts  1.24 us (3%)
    pallas_call x1, Pallas kernels, per_device(): pl.pallas_call(kernel, out_shape=jax.ShapeDtypeStruct((rows,), jnp.float3...  44.9 us
    unnamed x1, local copies, waits for them, and re-layouts  1.24 us

profile of v3, /device:TPU:1, one launch (start us, length us, event | category | flops | bytes accessed | tf_op | source)
XLA Modules:
  0.0 46.2 jit_solution(12427469408282811950)
XLA Ops:
  0.0 44.9 %shard_map.28 = f32[256]{0:T(256)} custom-call(bf16[256,1024]{1,0:T(8,128)(2,1)} %x_ref.1, s32[1,256]{1,0:T(1,128)} %bitcast.1), custom_call_target="tpu_custom_call" | custom-call | tf_op jit(solution)/shard_map/pallas_call | solution.py:286
  44.9 1.2 %copy.4 = f32[256]{0:T(256)} copy(f32[256]{0:T(256)} %shard_map.28) | data formatting | bytes 2048

commit v4 on v3

--- a/solution.py
+++ b/solution.py
@@ -24,18 +24,19 @@
 LAST_EITHER = ((1, 11), (12,))
 ARRIVING = ((1, 2, 3, 4), (5, 6), (7, 8, 9, 10, 11, 12))
 TOGETHER = ((0,), (1, 3, 4), (5, 6), (7, 10, 11))
+DONE_NEAR, DONE_FAR, DONE_LAST, DONE_FULL, DONE = (2,), (0, 3, 5, 8), (4, 6), (7, 9, 10), (1, 11, 12)
 SHARED = (0, 1, 3, 4, 5, 6, 7, 10, 11)
 
 K = len(SLOTS)
-BOUNDS = (0, 32, 64, 96, 128, 160, 192, 224, 256)
+BOUNDS = tuple(range(0, 257, 16))
 CHUNKS = len(BOUNDS) - 1
-HALFWAY = 4
-AHEAD = 3
-
-
-def kernel(x_ref, cluster_ref, out_ref, buf, cid, rid, rowacc, colacc, outb, inb,
+HALFWAY = 8
+AHEAD = 7
+
+
+def kernel(x_hbm, cluster_hbm, out_ref, x_ref, cluster_ref, buf, cid, rid, rowacc, colacc, outb, inb,
            arrive, shared, ids_in, ids_pair, sent, sent_pair, ids_sent, ids_pair_sent,
-           res_in, res_pair_in, res_sent, res_pair_sent):
+           res_in, res_pair_in, res_sent, res_pair_sent, loaded, loaded_ids):
     rows = x_ref.shape[0]
     half = rows // 2
     group, tile = lax.axis_index("group"), lax.axis_index("tile")
@@ -61,14 +62,24 @@
     for partner in partners:
         pl.semaphore_signal(barrier, inc=1, device_id=partner, device_id_type=MESH)
 
-    e32 = x_ref[...].astype(jnp.float32)
-    normed = e32 * lax.rsqrt(jnp.sum(e32 * e32, axis=1, keepdims=True) + EPS)
-    buf[0, core] = normed.astype(jnp.bfloat16)
-    cid[0, core] = cluster_ref[...]
-    rowacc[...] = jnp.full(rowacc.shape, -1.0, jnp.float32)
-    colacc[...] = jnp.full(colacc.shape, -1.0, jnp.float32)
-
-    pl.semaphore_wait(barrier, len(partners))
+    quarter = rows // 4
+
+    def load(q):
+        rows_of = pl.ds(q * quarter, quarter)
+        return pltpu.make_async_copy(x_hbm.at[rows_of], x_ref.at[rows_of], loaded.at[q])
+
+    load_ids = pltpu.make_async_copy(cluster_hbm, cluster_ref, loaded_ids)
+    load(0).start()
+    load_ids.start()
+    for q in range(1, 4):
+        load(q).start()
+
+    def normalise(q):
+        rows_of = pl.ds(q * quarter, quarter)
+        load(q).wait()
+        e32 = x_ref[rows_of].astype(jnp.float32)
+        normed = e32 * lax.rsqrt(jnp.sum(e32 * e32, axis=1, keepdims=True) + EPS)
+        buf[0, core, rows_of] = normed.astype(jnp.bfloat16)
 
     def remote(src, dst, send, recv, to):
         return pltpu.make_async_remote_copy(
@@ -100,9 +111,11 @@
     def whole(slot):
         return remote(buf.at[slot, core], buf.at[slot, core], sent_pair, shared.at[slot], sibling)
 
-    def whole_shared(*slots):
+    def paired_ids(*slots):
         some = pl.ds(0, len(slots))
         remote(cid.at[some, core], cid.at[some, core], ids_pair_sent, ids_pair.at[slots[0]], sibling).wait_recv()
+
+    def paired(*slots):
         for slot in slots:
             whole(slot).wait_recv()
 
@@ -162,17 +175,47 @@
     def halves(which, h):
         return [(i, h * half, half) for i in which]
 
+    def result(slot, which):
+        return remote(outb.at[slot, which], inb.at[slot, core], res_sent, res_in, device(owner(slot), which))
+
+    def result_pair():
+        return remote(outb.at[0, 1 - core], inb.at[0, core], res_pair_sent, res_pair_in, sibling)
+
+    def finish(slots):
+        for slot in slots:
+            down = jnp.max(colacc[slot], axis=0, keepdims=True)
+            outb[slot, 0] = down[:, :rows]
+            outb[slot, 1] = down[:, rows:]
+            along = jnp.max(rowacc[slot].T, axis=0, keepdims=True)
+            outb[slot, core] = jnp.maximum(outb[slot, core], along)
+            if slot == 0:
+                result_pair().start()
+            else:
+                for which in range(2):
+                    result(slot, which).start()
+
+    load_ids.wait()
+    cid[0, core] = cluster_ref[...]
+    normalise(0)
+    pl.semaphore_wait(barrier, len(partners))
     for dst in (1, 2, 3, 4):
         ids(edge_to[dst]).start()
-    for n in range(AHEAD):
+    for n in range(CHUNKS // 4):
         for dst in (1, 2):
             chunk(edge_to[dst], n).start()
-        if n == 0:
-            for dst in (3, 4):
-                part(edge_to[dst], 0).start()
+    normalise(1)
+    for dst in (3, 4):
+        part(edge_to[dst], 0).start()
+    normalise(2)
+    for n in range(CHUNKS // 4, AHEAD):
+        for dst in (1, 2):
+            chunk(edge_to[dst], n).start()
+    normalise(3)
     ids_across(0).start()
     for h in range(2):
         across(0, h).start()
+    rowacc[...] = jnp.full(rowacc.shape, -1.0, jnp.float32)
+    colacc[...] = jnp.full(colacc.shape, -1.0, jnp.float32)
     row_ids(0)
 
     for n in range(CHUNKS):
@@ -187,10 +230,11 @@
             chunk(edge_to[dst], n).start()
         if n == 0:
             got_ids(1, 2, 3, 4)
-        if n == 1:
+        if n == 2:
             for dst in (3, 4):
                 part(edge_to[dst], 1).start()
-            whole_shared(0)
+            paired_ids(0)
+            paired(0)
             compare(0, full((0,)), own=True)
         if n == HALFWAY:
             for dst in (3, 4):
@@ -212,7 +256,8 @@
         across(dst, 1).start()
     for dst in (5, 6):
         across(dst, 0).start()
-    whole_shared(1, 3, 4)
+    paired_ids(1, 3, 4)
+    paired(1, 3, 4)
     compare(NEAR[0][0], full(NEAR[0][1]))
     for dst in (5, 6):
         got(dst, 1)
@@ -223,9 +268,11 @@
     got_ids(7, 8, 9, 10, 11, 12)
     for j, which in NEAR[1:]:
         compare(j, full(which))
-    whole_shared(5, 6)
+    paired_ids(5, 6)
+    paired(5, 6)
     for j, which in RELAYED:
         compare(j, full(which))
+    finish(DONE_NEAR)
 
     for h in range(2):
         for dst in (7, 8, 9, 10):
@@ -234,34 +281,24 @@
             across(dst, h).start()
         for j, which in FAR:
             compare(j, halves(which, h))
+        if h == 1:
+            finish(DONE_FAR)
         for dst in (11, 12):
             got(dst, h)
         across(11, h).start()
         for j, which in LAST:
             compare(j, halves(which, h))
-    whole_shared(7, 10, 11)
+    finish(DONE_LAST)
+    paired_ids(7, 10, 11)
+    paired(7, 10)
     for j, which in LAST_FULL:
         compare(j, full(which))
+    finish(DONE_FULL)
+    paired(11)
     either, which = LAST_EITHER
     compare(jnp.where(here[0] // 2 == 0, *either), full(which))
 
-    def result(slot, which):
-        return remote(outb.at[slot, which], inb.at[slot, core], res_sent, res_in, device(owner(slot), which))
-
-    def result_pair():
-        return remote(outb.at[0, 1 - core], inb.at[0, core], res_pair_sent, res_pair_in, sibling)
-
-    for slot in range(K):
-        down = jnp.max(colacc[slot], axis=0, keepdims=True)
-        outb[slot, 0] = down[:, :rows]
-        outb[slot, 1] = down[:, rows:]
-        along = jnp.max(rowacc[slot].T, axis=0, keepdims=True)
-        outb[slot, core] = jnp.maximum(outb[slot, core], along)
-        if slot == 0:
-            result_pair().start()
-        else:
-            for which in range(2):
-                result(slot, which).start()
+    finish(DONE)
     result_pair().wait()
     everything = pltpu.make_async_remote_copy(
         src_ref=outb.at[pl.ds(1, K - 1)], dst_ref=inb.at[pl.ds(1, K - 1)], send_sem=res_sent, recv_sem=res_in,
@@ -270,7 +307,7 @@
     everything.wait_recv()
     best = jnp.maximum(outb[0, core], inb[0, 1 - core])
     best = jnp.maximum(best, jnp.max(jnp.max(inb[pl.ds(1, K - 1)], axis=0), axis=0))
-    out_ref[...] = jnp.maximum(best, -1.0)[0]
+    out_ref[...] = jnp.maximum(best, -1.0)
 
     everything.wait_send()
     every, across_all = pl.ds(0, len(FIRST + SECOND)), pl.ds(0, len(SHARED))
@@ -283,12 +320,14 @@
 def per_device(embeddings, cluster):
     rows, width = embeddings.shape
     dma = pltpu.SemaphoreType.DMA
-    return pl.pallas_call(
+    best = pl.pallas_call(
         kernel,
-        out_shape=jax.ShapeDtypeStruct((rows,), jnp.float32),
-        in_specs=[pl.BlockSpec(memory_space=pltpu.VMEM)] * 2,
+        out_shape=jax.ShapeDtypeStruct((1, rows), jnp.float32),
+        in_specs=[pl.BlockSpec(memory_space=pltpu.HBM)] * 2,
         out_specs=pl.BlockSpec(memory_space=pltpu.VMEM),
         scratch_shapes=[
+            pltpu.VMEM((rows, width), embeddings.dtype),
+            pltpu.VMEM((1, rows), jnp.int32),
             pltpu.VMEM((K, 2, rows, width), jnp.bfloat16),
             pltpu.VMEM((K, 2, 1, rows), jnp.int32),
             pltpu.VMEM((K, rows, 128), jnp.int32),
@@ -297,12 +336,13 @@
             pltpu.VMEM((K, 2, 1, rows), jnp.float32),
             pltpu.VMEM((K, 2, 1, rows), jnp.float32),
             dma((2 * CHUNKS + 2 * (K - 3),)), dma((K,)), dma((K,)), dma((K,)), dma, dma, dma, dma,
-            dma, dma, dma, dma,
+            dma, dma, dma, dma, dma((4,)), dma,
         ],
         compiler_params=pltpu.CompilerParams(
             collective_id=0, has_side_effects=True, vmem_limit_bytes=56 * 2**20
         ),
     )(embeddings, cluster.reshape(1, rows))
+    return best.reshape(rows)
 
 
 def solution(mesh):

time: 46.3 us -> 44.8 us (0.968)
  Pallas kernels: 44.9 us -> 43.4 us
    pallas_call x1, Pallas kernels: 44.9 us -> 43.4 us  [per_device(): pl.pallas_call(kernel, out_shape=jax.ShapeDtypeStruct((1, rows), jnp.floa...]
    unnamed x1 -> x3, local copies, waits for them, and re-layouts: 1.24 us -> 1.22 us
where the time goes in v4:
time: 44.8 us; the launch traced here: 44.7 us
  Pallas kernels  43.4 us (97%)
  local copies, waits for them, and re-layouts  1.22 us (3%)
    pallas_call x1, Pallas kernels, per_device(): pl.pallas_call(kernel, out_shape=jax.ShapeDtypeStruct((1, rows), jnp.floa...  43.4 us
    unnamed x3, local copies, waits for them, and re-layouts  1.22 us

profile of v4, /device:TPU:1, one launch (start us, length us, event | category | flops | bytes accessed | tf_op | source)
XLA Modules:
  0.0 44.7 jit_solution(11517369436424015712)
XLA Ops:
  0.0 43.4 %shard_map.28 = f32[1,256]{1,0:T(1,128)} custom-call(bf16[256,1024]{1,0:T(8,128)(2,1)} %x_hbm.1, s32[1,256]{1,0:T(1,128)} %bitcast.3), custom_call_target="tpu_custom_call" | custom-call | tf_op jit(solution)/shard_map/pallas_call | solution.py:323
  43.4 0.0 copy-start
  43.4 0.7 %copy-done = f32[1,256]{1,0:T(1,128)S(1)} copy-done((f32[1,256]{1,0:T(1,128)S(1)}, f32[1,256]{1,0:T(1,128)}, u32[]{:S(2)}) %copy-start) | copy-done | bytes 1048
  44.1 0.6 %copy.4 = f32[256]{0:T(256)} copy(f32[256]{0:T(256)S(1)} %bitcast.2) | data formatting | bytes 2048
Async XLA Ops:
  43.4 0.7 %copy-start = (f32[1,256]{1,0:T(1,128)S(1)}, f32[1,256]{1,0:T(1,128)}, u32[]{:S(2)}) copy-start(f32[1,256]{1,0:T(1,128)} %shard_map.28) | copy-start | bytes 3076

commit v5 on v4

--- a/solution.py
+++ b/solution.py
@@ -16,21 +16,22 @@
 )
 FIRST = ((0, 1, 0), (0, 2, 1), (0, 3, 2), (0, 4, 4), (1, 5, 3), (2, 6, 5))
 SECOND = ((3, 7, 0), (3, 8, 1), (3, 9, 2), (4, 10, 4), (5, 11, 3), (6, 12, 5))
+DETOUR = ((9, 11, 0), (10, 12, 1))
+HEAD = 32
 NEAR = ((4, (0, 2, 3)), (3, (0, 2, 1)), (1, (0, 2, 4)))
 RELAYED = ((5, (3, 4, 2)), (6, (4, 3, 1, 5)))
-FAR = ((0, (10, 9)), (4, (9, 7, 8)), (3, (10,)), (5, (10, 8)), (6, (8, 9, 7)))
-LAST = ((4, (11,)), (6, (11,)))
+FAR = ((0, (10, 9)), (3, (10,)), (5, (10, 8)))
+LAST = ((4, (9, 7, 8, 11)), (6, (8, 9, 7, 11)))
 LAST_FULL = ((10, (9, 7, 11)), (7, (12,)))
 LAST_EITHER = ((1, 11), (12,))
 ARRIVING = ((1, 2, 3, 4), (5, 6), (7, 8, 9, 10, 11, 12))
 TOGETHER = ((0,), (1, 3, 4), (5, 6), (7, 10, 11))
-DONE_NEAR, DONE_FAR, DONE_LAST, DONE_FULL, DONE = (2,), (0, 3, 5, 8), (4, 6), (7, 9, 10), (1, 11, 12)
 SHARED = (0, 1, 3, 4, 5, 6, 7, 10, 11)
 
 K = len(SLOTS)
 BOUNDS = tuple(range(0, 257, 16))
 CHUNKS = len(BOUNDS) - 1
-HALFWAY = 8
+SPLIT = 128
 AHEAD = 7
 
 
@@ -38,7 +39,8 @@
            arrive, shared, ids_in, ids_pair, sent, sent_pair, ids_sent, ids_pair_sent,
            res_in, res_pair_in, res_sent, res_pair_sent, loaded, loaded_ids):
     rows = x_ref.shape[0]
-    half = rows // 2
+    limits = (0, SPLIT, rows)
+    halfway = BOUNDS.index(SPLIT)
     group, tile = lax.axis_index("group"), lax.axis_index("tile")
     core = lax.rem(group, 2)
     here = (group // 2, tile // 4, lax.rem(tile, 4))
@@ -95,17 +97,23 @@
 
     def chunk(edge, n):
         dst = edge[1]
-        sem = arrive.at[(dst - 1) * CHUNKS + n if dst in (1, 2) else 2 * CHUNKS + 2 * (dst - 3) + n // HALFWAY]
+        sem = arrive.at[(dst - 1) * CHUNKS + n if dst in (1, 2) else 2 * CHUNKS + 2 * (dst - 3) + n // halfway]
         return move(edge, piece(BOUNDS[n], BOUNDS[n + 1]), sem)
 
     def part(edge, h):
-        return move(edge, piece(h * half, (h + 1) * half), arrive.at[2 * CHUNKS + 2 * (edge[1] - 3) + h])
+        begin = HEAD if edge[1] in (11, 12) and h == 0 else limits[h]
+        return move(edge, piece(begin, limits[h + 1]), arrive.at[2 * CHUNKS + 2 * (edge[1] - 3) + h])
+
+    def detour(edge):
+        return move(edge, piece(0, HEAD), arrive.at[2 * CHUNKS + 2 * (K - 3) + edge[1] - 11])
 
     def got(slot, h):
         part((0, slot, 0), h).wait_recv()
 
     def across(slot, h):
-        rows_of = piece(h * half, (h + 1) * half)
+        return across_rows(slot, piece(HEAD if slot == 11 and h == 0 else limits[h], limits[h + 1]))
+
+    def across_rows(slot, rows_of):
         return remote(buf.at[slot, core, rows_of], buf.at[slot, core, rows_of], sent_pair, shared.at[slot], sibling)
 
     def whole(slot):
@@ -173,7 +181,7 @@
         return [(i, 0, rows) for i in which]
 
     def halves(which, h):
-        return [(i, h * half, half) for i in which]
+        return [(i, limits[h], limits[h + 1] - limits[h]) for i in which]
 
     def result(slot, which):
         return remote(outb.at[slot, which], inb.at[slot, core], res_sent, res_in, device(owner(slot), which))
@@ -222,9 +230,6 @@
         for dst in (1, 2):
             if n + AHEAD < CHUNKS:
                 chunk(edge_to[dst], n + AHEAD).start()
-        if n + AHEAD == CHUNKS:
-            for dst in (7, 8):
-                part(edge_to[dst], 0).start()
         for src, dst in ((1, 5), (2, 6)):
             chunk(edge_to[src], n).wait_recv()
             chunk(edge_to[dst], n).start()
@@ -236,10 +241,10 @@
             paired_ids(0)
             paired(0)
             compare(0, full((0,)), own=True)
-        if n == HALFWAY:
+        if n == halfway:
             for dst in (3, 4):
                 got(dst, 0)
-            for dst in (9, 10):
+            for dst in (7, 8, 9, 10):
                 part(edge_to[dst], 0).start()
             for dst in (1, 3, 4):
                 across(dst, 0).start()
@@ -272,33 +277,41 @@
     paired(5, 6)
     for j, which in RELAYED:
         compare(j, full(which))
-    finish(DONE_NEAR)
+    finish((2,))
 
     for h in range(2):
         for dst in (7, 8, 9, 10):
             got(dst, h)
+        if h == 0:
+            for edge in DETOUR:
+                detour(edge).start()
         for dst in (7, 10):
             across(dst, h).start()
         for j, which in FAR:
             compare(j, halves(which, h))
-        if h == 1:
-            finish(DONE_FAR)
         for dst in (11, 12):
             got(dst, h)
+        if h == 1:
+            for edge in DETOUR:
+                detour(edge).wait_recv()
+            across_rows(11, piece(0, HEAD)).start()
         across(11, h).start()
         for j, which in LAST:
-            compare(j, halves(which, h))
-    finish(DONE_LAST)
+            pieces = halves([i for i in which if i != 11], h)
+            if h == 0:
+                pieces += [(11, HEAD, SPLIT - HEAD)]
+            else:
+                pieces += [(11, SPLIT, rows - SPLIT), (11, 0, HEAD)]
+            compare(j, pieces)
     paired_ids(7, 10, 11)
     paired(7, 10)
     for j, which in LAST_FULL:
         compare(j, full(which))
-    finish(DONE_FULL)
     paired(11)
     either, which = LAST_EITHER
     compare(jnp.where(here[0] // 2 == 0, *either), full(which))
-
-    finish(DONE)
+    finish((11, 12, 10, 9, 8, 7, 6, 5, 1, 3, 4, 0))
+
     result_pair().wait()
     everything = pltpu.make_async_remote_copy(
         src_ref=outb.at[pl.ds(1, K - 1)], dst_ref=inb.at[pl.ds(1, K - 1)], send_sem=res_sent, recv_sem=res_in,
@@ -335,7 +348,7 @@
             pltpu.VMEM((K, 8, 2 * rows), jnp.float32),
             pltpu.VMEM((K, 2, 1, rows), jnp.float32),
             pltpu.VMEM((K, 2, 1, rows), jnp.float32),
-            dma((2 * CHUNKS + 2 * (K - 3),)), dma((K,)), dma((K,)), dma((K,)), dma, dma, dma, dma,
+            dma((2 * CHUNKS + 2 * (K - 3) + 2,)), dma((K,)), dma((K,)), dma((K,)), dma, dma, dma, dma,
             dma, dma, dma, dma, dma((4,)), dma,
         ],
         compiler_params=pltpu.CompilerParams(

time: 44.8 us -> 44.4 us (level)
  no operation moved by 1% of the time
where the time goes in v5:
time: 44.4 us; the launch traced here: 44.3 us
  Pallas kernels  43 us (97%)
  local copies, waits for them, and re-layouts  1.22 us (3%)
    pallas_call x1, Pallas kernels, per_device(): pl.pallas_call(kernel, out_shape=jax.ShapeDtypeStruct((1, rows), jnp.floa...  43 us
    unnamed x3, local copies, waits for them, and re-layouts  1.22 us

profile of v5, /device:TPU:1, one launch (start us, length us, event | category | flops | bytes accessed | tf_op | source)
XLA Modules:
  0.0 44.3 jit_solution(13830681567396664420)
XLA Ops:
  0.0 43.0 %shard_map.28 = f32[1,256]{1,0:T(1,128)} custom-call(bf16[256,1024]{1,0:T(8,128)(2,1)} %x_hbm.1, s32[1,256]{1,0:T(1,128)} %bitcast.3), custom_call_target="tpu_custom_call" | custom-call | tf_op jit(solution)/shard_map/pallas_call | solution.py:336
  43.0 0.0 copy-start
  43.0 0.7 %copy-done = f32[1,256]{1,0:T(1,128)S(1)} copy-done((f32[1,256]{1,0:T(1,128)S(1)}, f32[1,256]{1,0:T(1,128)}, u32[]{:S(2)}) %copy-start) | copy-done | bytes 1048
  43.7 0.6 %copy.4 = f32[256]{0:T(256)} copy(f32[256]{0:T(256)S(1)} %bitcast.2) | data formatting | bytes 2048
Async XLA Ops:
  43.0 0.7 %copy-start = (f32[1,256]{1,0:T(1,128)S(1)}, f32[1,256]{1,0:T(1,128)}, u32[]{:S(2)}) copy-start(f32[1,256]{1,0:T(1,128)} %shard_map.28) | copy-start | bytes 3076

commit v6 on v5

--- a/solution.py
+++ b/solution.py
@@ -22,7 +22,8 @@
 RELAYED = ((5, (3, 4, 2)), (6, (4, 3, 1, 5)))
 FAR = ((0, (10, 9)), (3, (10,)), (5, (10, 8)))
 LAST = ((4, (9, 7, 8, 11)), (6, (8, 9, 7, 11)))
-LAST_FULL = ((10, (9, 7, 11)), (7, (12,)))
+BEFORE_LAST = ((10, (9, 7)),)
+LAST_FULL = ((10, (11,)), (7, (12,)))
 LAST_EITHER = ((1, 11), (12,))
 ARRIVING = ((1, 2, 3, 4), (5, 6), (7, 8, 9, 10, 11, 12))
 TOGETHER = ((0,), (1, 3, 4), (5, 6), (7, 10, 11))
@@ -289,6 +290,11 @@
             across(dst, h).start()
         for j, which in FAR:
             compare(j, halves(which, h))
+        if h == 1:
+            paired_ids(7, 10, 11)
+            paired(7, 10)
+            for j, which in BEFORE_LAST:
+                compare(j, full(which))
         for dst in (11, 12):
             got(dst, h)
         if h == 1:
@@ -303,8 +309,6 @@
             else:
                 pieces += [(11, SPLIT, rows - SPLIT), (11, 0, HEAD)]
             compare(j, pieces)
-    paired_ids(7, 10, 11)
-    paired(7, 10)
     for j, which in LAST_FULL:
         compare(j, full(which))
     paired(11)

time: 44.4 us -> 44 us (level)
  no operation moved by 1% of the time
where the time goes in v6:
time: 44 us; the launch traced here: 43.9 us
  Pallas kernels  42.7 us (97%)
  local copies, waits for them, and re-layouts  1.22 us (3%)
    pallas_call x1, Pallas kernels, per_device(): pl.pallas_call(kernel, out_shape=jax.ShapeDtypeStruct((1, rows), jnp.floa...  42.7 us
    unnamed x3, local copies, waits for them, and re-layouts  1.22 us

profile of v6, /device:TPU:1, one launch (start us, length us, event | category | flops | bytes accessed | tf_op | source)
XLA Modules:
  0.0 43.9 jit_solution(2515392055485056929)
XLA Ops:
  0.0 42.7 %shard_map.28 = f32[1,256]{1,0:T(1,128)} custom-call(bf16[256,1024]{1,0:T(8,128)(2,1)} %x_hbm.1, s32[1,256]{1,0:T(1,128)} %bitcast.3), custom_call_target="tpu_custom_call" | custom-call | tf_op jit(solution)/shard_map/pallas_call | solution.py:340
  42.7 0.0 copy-start
  42.7 0.7 %copy-done = f32[1,256]{1,0:T(1,128)S(1)} copy-done((f32[1,256]{1,0:T(1,128)S(1)}, f32[1,256]{1,0:T(1,128)}, u32[]{:S(2)}) %copy-start) | copy-done | bytes 1048
  43.3 0.6 %copy.4 = f32[256]{0:T(256)} copy(f32[256]{0:T(256)S(1)} %bitcast.2) | data formatting | bytes 2048
Async XLA Ops:
  42.7 0.7 %copy-start = (f32[1,256]{1,0:T(1,128)S(1)}, f32[1,256]{1,0:T(1,128)}, u32[]{:S(2)}) copy-start(f32[1,256]{1,0:T(1,128)} %shard_map.28) | copy-start | bytes 3076
